TPU v7x, 32 devices: a whole 2x2x4 slice. The times are simulated.
32 devices in a mesh: case: 2 (over x), span: 16 (over z, y, core).
Axes of the slice: x: 2, y: 2, z: 4, core: 2. Of those that a mesh axis runs over, the one named last changes fastest.
Arguments:
- adjoint_in: float32 [38, 16, 128, 128], P('case', 'span'), parts along dimension 0, may hold values from -6 to 6
- density: float32 [4, 16, 128, 128], P('case', 'span'), parts along dimension 0, may hold values from 0.8 to 1.2
- velocity: float32 [4, 3, 16, 128, 128], P('case', None, 'span'), parts along dimension 0, may hold values from -0.25 to 0.25
- links: int32 [2, 32, 128, 128], P(None, ('case', 'span')), parts along dimension 1, may hold values from 0 to 1023, as said below
- patch_map: int32 [32, 128, 128], P(('case', 'span')), parts along dimension 0, may hold values from 0 to 4095
- owner: int32 [4096], replicated, may hold values from 0 to 4095, each once
- relax: float32 [38], P('case'), parts along dimension 0, may hold values from 0.5 to 1.9
Outputs:
- adjoint_out: float32 [38, 16, 128, 128], P('case', 'span'), parts along dimension 0
- patch_gradient: float32 [8192], P(('case', 'span')), parts along dimension 0
There are 2 independent parts, one for each index of `case`. A program takes and returns all parts, laid end to end along the dimension named above; an argument that names none is the same for every part. Nothing has to cross between parts.
Inputs may be any that keep to these rules, and one draw needn't show every extreme that they name: `links`: bit j of a cell (held in plane j // 10 at position j mod 10) is set exactly when the cell at x + c_j is solid (bit 0: the cell itself); cells beyond the cross-section count as solid, the span is periodic. The solid body is a cylinder with a helical fillet. `patch_map`: patch of every cell; only cells with some link bit set contribute.
All inputs are finite; a program needn't handle non-finite values.
Results may differ from a plain program's by a relative error of at most 0.00013.
Values sent between devices are 32-bit elements; how exact they have to be, the bound alone decides.
A program may use at most 64 MiB of HBM per device.

v0:
```python
import jax
import jax.numpy as jnp
from jax import lax
from jax.sharding import PartitionSpec as P


def padded_2(block, sides, width):
    for axis, dim in sides:
        count = lax.axis_size(axis)
        forward = [(i, i + 1) for i in range(count - 1)]
        forward.append((count - 1, 0))
        backward = [(target, source) for source, target in forward]
        low = lax.ppermute(
            lax.slice_in_dim(block, block.shape[dim] - width, None, axis=dim), axis, forward
        )
        high = lax.ppermute(lax.slice_in_dim(block, 0, width, axis=dim), axis, backward)
        block = jnp.concatenate([low, block, high], axis=dim)
    return block


def lattice_tables():
    velocities = [
        [0, 0, 0],
        [1, 0, 0],
        [-1, 0, 0],
        [0, 1, 0],
        [0, -1, 0],
        [0, 0, 1],
        [0, 0, -1],
        [1, 1, 0],
        [-1, -1, 0],
        [1, -1, 0],
        [-1, 1, 0],
        [1, 0, 1],
        [-1, 0, -1],
        [1, 0, -1],
        [-1, 0, 1],
        [0, 1, 1],
        [0, -1, -1],
        [0, 1, -1],
        [0, -1, 1],
    ]
    weights = [1.0 / 3.0] + [1.0 / 18.0] * 6 + [1.0 / 36.0] * 12
    opposite = [0, 2, 1, 4, 3, 6, 5, 8, 7, 10, 9, 12, 11, 14, 13, 16, 15, 18, 17]
    lattice = jnp.asarray(velocities, jnp.float32)
    along_x = lattice[:, 0]
    along_y = lattice[:, 1]
    along_z = lattice[:, 2]
    monomials = [
        jnp.ones((19,), jnp.float32),
        along_x,
        along_y,
        along_z,
        along_x * along_y,
        along_x * along_z,
        along_y * along_z,
        along_x * along_x,
        along_y * along_y,
        along_z * along_z,
        along_x * along_y * along_y,
        along_x * along_z * along_z,
        along_y * along_x * along_x,
        along_z * along_x * along_x,
        along_y * along_z * along_z,
        along_z * along_y * along_y,
        along_x * along_x * along_y * along_y,
        along_x * along_x * along_z * along_z,
        along_y * along_y * along_z * along_z,
    ]
    basis = []
    for column in monomials:
        vector = column
        for sweep in range(2):
            for earlier in basis:
                vector = vector - jnp.sum(vector * earlier) * earlier
        vector = vector / jnp.sqrt(jnp.sum(vector * vector))
        basis.append(vector)
    return (velocities, weights, opposite, jnp.stack(basis))


def link_bit(links, direction):
    return jnp.bitwise_and(jnp.right_shift(links[direction // 10], direction % 10), 1)


def shift_cross(plane, step_y, step_z):
    padded = jnp.pad(plane, ((0, 0), (1, 1), (1, 1)))
    return padded[
        :, 1 + step_y : 1 + step_y + plane.shape[1], 1 + step_z : 1 + step_z + plane.shape[2]
    ]


def collide_adjoint(propagated, velocity, fluid_mask, relax_rates):
    velocities, weights, opposite, moment_table = lattice_tables()
    highest = lax.Precision.HIGHEST
    full_shape = propagated.shape
    flattened = propagated.reshape(19, -1)
    flow_flat = velocity.reshape(3, -1)
    lattice = jnp.asarray(velocities, jnp.float32)
    moments = jnp.dot(moment_table, flattened, precision=highest)
    relaxed = jnp.dot(moment_table.T, relax_rates[:, None] * moments, precision=highest)
    projected = jnp.dot(lattice, flow_flat, precision=highest)
    speed_sq = jnp.sum(flow_flat * flow_flat, axis=0)
    weighted = jnp.asarray(weights, jnp.float32)[:, None] * relaxed
    scalar_part = jnp.sum(
        weighted * (1.0 - 4.5 * projected * projected + 1.5 * speed_sq[None, :]), axis=0
    )
    vector_part = (
        3.0 * jnp.dot(lattice.T, weighted * (1.0 + 3.0 * projected), precision=highest)
        - 3.0 * flow_flat * jnp.sum(weighted, axis=0)[None, :]
    )
    result = (
        flattened
        - relaxed
        + scalar_part[None, :]
        + jnp.dot(lattice, vector_part, precision=highest)
    )
    return (fluid_mask.reshape(1, -1) * result).reshape(full_shape)


def span_rims(adjoint):
    rising = [1, 7, 9, 11, 13]
    falling = [2, 8, 10, 12, 14]
    moving = jnp.stack([adjoint[index] for index in rising + falling])
    extended = padded_2(moving, (("span", 1),), 1)
    above = extended[:5, -1:]
    below = extended[5:, :1]
    return (above, below)


def reverse_step(adjoint, links, density, velocity, relax_rates):
    velocities, weights, opposite, moment_table = lattice_tables()
    rising = [1, 7, 9, 11, 13]
    falling = [2, 8, 10, 12, 14]
    above, below = span_rims(adjoint)
    fluid_mask = (1 - link_bit(links, 0)).astype(jnp.float32)
    speed_sq = jnp.sum(velocity * velocity, axis=0)
    propagated = []
    wall_term = jnp.zeros(links.shape[1:], jnp.float32)
    for direction in range(19):
        step_x = velocities[direction][0]
        step_y = velocities[direction][1]
        step_z = velocities[direction][2]
        if step_x == 1:
            shifted = jnp.concatenate(
                [adjoint[direction, 1:], above[rising.index(direction)]], axis=0
            )
        elif step_x == -1:
            shifted = jnp.concatenate(
                [below[falling.index(direction)], adjoint[direction, :-1]], axis=0
            )
        else:
            shifted = adjoint[direction]
        linked = link_bit(links, direction).astype(jnp.float32)
        upstream = shift_cross(shifted, step_y, step_z)
        reflected = adjoint[opposite[direction]]
        propagated.append(fluid_mask * ((1.0 - linked) * upstream + linked * reflected))
        along = step_x * velocity[0] + step_y * velocity[1] + step_z * velocity[2]
        equilibrium = density * (1.0 + 3.0 * along + 4.5 * along * along - 1.5 * speed_sq)
        wall_term = wall_term + fluid_mask * linked * equilibrium * reflected
    propagated = jnp.stack(propagated)
    return (collide_adjoint(propagated, velocity, fluid_mask, relax_rates), wall_term)


def body(adjoint_in, density, velocity, links, patch_map, owner, relax):
    relax_rates = relax * (jnp.arange(19) >= 4).astype(jnp.float32)
    adjoint = adjoint_in
    wall_total = jnp.zeros(links.shape[1:], jnp.float32)
    for time_level in (1, 0):
        adjoint, wall_term = reverse_step(
            adjoint, links, density[time_level], velocity[time_level], relax_rates
        )
        wall_total = wall_total + wall_term
    target_rows = jnp.take(owner, patch_map)
    local_sums = jax.ops.segment_sum(
        wall_total.reshape(-1), target_rows.reshape(-1), num_segments=owner.shape[0]
    )
    gradient = lax.psum_scatter(local_sums, "span", scatter_dimension=0, tiled=True)
    return (adjoint, gradient)


def solution(mesh):
    in_specs = (
        P("case", "span", None, None),
        P("case", "span", None, None),
        P("case", None, "span", None, None),
        P(None, ("case", "span"), None, None),
        P(("case", "span"), None, None),
        P(),
        P("case"),
    )
    out_specs = (P("case", "span", None, None), P(("case", "span")))
    return jax.shard_map(body, mesh=mesh, in_specs=in_specs, out_specs=out_specs, check_vma=False)
```

profile of v0, /device:TPU:1, one launch (start us, length us, event | category | flops | bytes accessed | tf_op | source)
XLA Modules:
  0.0 311.6 jit_solution(18335385045126339143)
XLA Ops:
  0.7 1.5 slice_dynamic-update-slice_fusion.9
  2.2 1.5 slice_dynamic-update-slice_fusion.8
  3.7 1.5 slice_dynamic-update-slice_fusion.7
  5.2 1.5 slice_dynamic-update-slice_fusion.6
  6.6 1.5 slice_dynamic-update-slice_fusion.5
  8.1 1.5 slice_dynamic-update-slice_fusion.4
  9.6 1.5 slice_dynamic-update-slice_fusion.3
  11.0 1.5 slice_dynamic-update-slice_fusion.2
  12.5 1.5 slice_dynamic-update-slice_fusion.1
  14.0 1.5 slice_dynamic-update-slice_fusion
  15.5 2.6 collective-permute-start.1
  19.5 90.5 %gather_fusion = s32[16384]{0:T(1024)S(1)} fusion(s32[4096]{0:T(1024)S(1)} %copy-done, s32[16384]{0:T(1024)S(1)} %bitcast_clamp_fusion), kind=kCustom, calls=%fused_computation | custom fusion | bytes 196608 | tf_op jit(solution)/shard_map/jit(_take)/gather | solution.py:173
  111.3 0.6 fusion.457
  112.0 1.0 multiply_multiply_fusion.41
  113.8 0.9 slice_bitcast_fusion.17
  115.2 3.7 %fusion.19 = f32[19,16384]{1,0:T(8,128)S(1)} fusion(f32[19,19]{1,0:T(8,128)S(1)} %copy-done.55, f32[16384]{0:T(1024)S(1)} %bitcast.1094, f32[19]{0:T(128)S(1)} %copy-done.96, f32[16384]{0:T(1024)S(1)} %bitcast.1092, f32[19]{0:T(128)S(1)} %copy-done.94, f32[16384]{0:T(1024)S(1)} %bitcast.1098, f32[19]{0:T(128)S(1)} %copy-done.92, f32[16384]{0:T(1024)S(1)} %bitcast.1096, ...), kind=kOutput, calls=%fused_computation.45 | convolution fusion | flops 82804736 | bytes 2493332 | tf_op jit(solution)/shard_map/dot_general | solution.py:100
  119.0 2.6 fusion.9
  121.6 2.1 fusion.5
  123.7 6.4 %stack.192 = f32[19,16384]{1,0:T(8,128)} concatenate(f32[1,16384]{1,0:T(1,128)} %bitcast.1085, f32[1,16384]{1,0:T(1,128)} %bitcast.1089, f32[1,16384]{1,0:T(1,128)} %bitcast.1087, f32[1,16384]{1,0:T(1,128)} %bitcast.1091, f32[1,16384]{1,0:T(1,128)} %bitcast.1111, f32[1,16384]{1,0:T(1,128)} %bitcast.1113, f32[1,16384]{1,0:T(1,128)} %bitcast.1115, f32[1,16384]{1,0:T(1,128)} %bitcast.1121, ...), dimensions={0} | concatenate | bytes 2490368 | tf_op jit(solution)/shard_map/stack | solution.py:160
  130.2 2.9 fusion.1
  133.1 1.1 fusion.517
  140.6 2.9 collective-permute-start.2
  143.5 1.7 fusion.143
  145.2 85.9 %scatter_custom_fusion = f32[4096]{0:T(1024)S(1)} fusion(s32[16384]{0:T(1024)} %fusion.457, f32[16384]{0:T(1024)} %fusion.143, f32[]{:T(128)} %constant.27.clone.1), kind=kCustom, calls=%fused_computation.811 | custom fusion | flops 16384 | bytes 16896 | tf_op jit(solution)/shard_map/scatter-add | solution.py:174
  231.2 61.3 %all-reduce.32 = f32[4096]{0:T(1024)S(1)} all-reduce(f32[4096]{0:T(1024)S(1)} %scatter_custom_fusion), channel_id=2, replica_groups=mesh['case'=2,'span'=16] {'span'}, use_global_device_ids=true, to_apply=%region_727.728.clone | all-reduce | flops 4096 | bytes 32768
  293.3 1.2 fusion.446
  295.6 3.5 %fusion.15 = f32[19,16384]{1,0:T(8,128)S(1)} fusion(f32[19,19]{1,0:T(8,128)S(1)} %copy-done.56, f32[16384]{0:T(1024)S(1)} %bitcast.1124, f32[16384]{0:T(1024)S(1)} %bitcast.1122, f32[16384]{0:T(1024)S(1)} %bitcast.1068, f32[16384]{0:T(1024)S(1)} %bitcast.1066, f32[16384]{0:T(1024)S(1)} %bitcast.1134, f32[16384]{0:T(1024)S(1)} %bitcast.1132, ...), kind=kOutput, calls=%fused_computation.24 | convolution fusion | flops 82804736 | bytes 2493332 | tf_op jit(solution)/shard_map/dot_general | solution.py:100
  299.3 2.5 fusion.13
  301.9 1.4 fusion.3
  303.3 4.5 %stack.215 = f32[19,16384]{1,0:T(8,128)S(1)} concatenate(f32[1,16384]{1,0:T(1,128)} %bitcast.1063, f32[1,16384]{1,0:T(1,128)} %bitcast.1061, f32[1,16384]{1,0:T(1,128)} %bitcast.1065, f32[1,16384]{1,0:T(1,128)} %bitcast.1073, f32[1,16384]{1,0:T(1,128)} %bitcast.1075, f32[1,16384]{1,0:T(1,128)} %bitcast.1127, f32[1,16384]{1,0:T(1,128)} %bitcast.1129, f32[1,16384]{1,0:T(1,128)} %bitcast.1077, ...), dimensions={0} | concatenate | bytes 2490368 | tf_op jit(solution)/shard_map/stack | solution.py:160
  307.8 2.4 fusion
  310.5 1.1 bitcast_bitcast_fusion
  (231 shorter events, 10.8 us)
Async XLA Ops:
  0.6 18.9 %copy-start = (s32[4096]{0:T(1024)S(1)}, s32[4096]{0:T(1024)}, u32[]{:S(2)}) copy-start(s32[4096]{0:T(1024)} %param.18) | copy-start | bytes 49156
  0.6 17.5 %copy-start.3 = (f32[2,3,1,128,128]{4,3,2,1,0:T(8,128)S(1)}, f32[2,3,1,128,128]{4,3,2,1,0:T(8,128)}, u32[]{:S(2)}) copy-start(f32[2,3,1,128,128]{4,3,2,1,0:T(8,128)} %param.15) | copy-start | bytes 1179652
  0.7 18.1 %copy-start.1 = (s32[2,1,128,128]{3,2,1,0:T(8,128)S(1)}, s32[2,1,128,128]{3,2,1,0:T(8,128)}, u32[]{:S(2)}) copy-start(s32[2,1,128,128]{3,2,1,0:T(8,128)} %param.16) | copy-start | bytes 393220
  0.7 18.1 %copy-start.43 = (s32[1,128,128]{2,1,0:T(8,128)S(1)}, s32[1,128,128]{2,1,0:T(8,128)}, u32[]{:S(2)}) copy-start(s32[1,128,128]{2,1,0:T(8,128)} %param.17) | copy-start | bytes 196612
  15.5 96.5 %collective-permute-start = (f32[10,1,128,128]{3,2,1,0:T(8,128)}, f32[10,1,128,128]{3,2,1,0:T(8,128)}, u32[]{:S(2)}, u32[]{:S(2)}) collective-permute-start(f32[10,1,128,128]{3,2,1,0:T(8,128)} %slice_dynamic-update-slice_fusion), channel_id=1, source_target_pairs={{1,0},{2,1},{3,2},{4,3},{5,4},{6,5},{7,6},{8,7},{9,8},{10,9},{11,1... | collective-permute-start | bytes 1966088 | tf_op jit(solution)/shard_map/ppermute | solution.py:16
  15.5 96.5 %collective-permute-start.1 = (f32[10,1,128,128]{3,2,1,0:T(8,128)}, f32[10,1,128,128]{3,2,1,0:T(8,128)S(1)}, u32[]{:S(2)}, u32[]{:S(2)}) collective-permute-start(f32[10,1,128,128]{3,2,1,0:T(8,128)} %slice_dynamic-update-slice_fusion), channel_id=1, source_target_pairs={{0,1},{1,2},{2,3},{3,4},{4,5},{5,6},{6,7},{7,8},{8,9},{9,10},{10,1... | collective-permute-start | bytes 1966088 | tf_op jit(solution)/shard_map/ppermute | solution.py:13
  18.1 91.9 %copy-start.6 = (f32[128,128]{1,0:T(8,128)}, f32[128,128]{1,0:T(8,128)S(1)}, u32[]{:S(2)}) copy-start(f32[128,128]{1,0:T(8,128)S(1)} %get-tuple-element.13) | copy-start | bytes 196612
  19.5 90.6 %copy-start.57 = (u32[32]{0:T(128)S(1)}, u32[32]{0:T(128)}, u32[]{:S(2)}) copy-start(u32[32]{0:T(128)} %constant.2367) | copy-start | bytes 388
  19.5 91.8 %copy-start.54 = (f32[19]{0:T(128)S(1)}, f32[19]{0:T(128)}, u32[]{:S(2)}) copy-start(f32[19]{0:T(128)} %param.19) | copy-start | bytes 232
  19.5 92.5 %copy-start.2 = (f32[19,1,128,128]{3,2,1,0:T(8,128)S(1)}, f32[19,1,128,128]{3,2,1,0:T(8,128)}, u32[]{:S(2)}) copy-start(f32[19,1,128,128]{3,2,1,0:T(8,128)} %param.13) | copy-start | bytes 3735556
  113.7 5.2 %copy-start.32 = (f32[1,128,128]{2,1,0:T(8,128)}, f32[1,128,128]{2,1,0:T(8,128)S(1)}, u32[]{:S(2)}) copy-start(f32[1,128,128]{2,1,0:T(8,128)S(1)} %get-tuple-element.47) | copy-start | bytes 196612
  113.7 5.2 %copy-start.33 = (f32[1,128,128]{2,1,0:T(8,128)}, f32[1,128,128]{2,1,0:T(8,128)S(1)}, u32[]{:S(2)}) copy-start(f32[1,128,128]{2,1,0:T(8,128)S(1)} %get-tuple-element.48) | copy-start | bytes 196612
  113.7 5.2 %copy-start.34 = (f32[1,128,128]{2,1,0:T(8,128)}, f32[1,128,128]{2,1,0:T(8,128)S(1)}, u32[]{:S(2)}) copy-start(f32[1,128,128]{2,1,0:T(8,128)S(1)} %get-tuple-element.49) | copy-start | bytes 196612
  113.7 5.2 %copy-start.35 = (f32[1,128,128]{2,1,0:T(8,128)}, f32[1,128,128]{2,1,0:T(8,128)S(1)}, u32[]{:S(2)}) copy-start(f32[1,128,128]{2,1,0:T(8,128)S(1)} %get-tuple-element.50) | copy-start | bytes 196612
  113.7 5.2 %copy-start.36 = (f32[1,128,128]{2,1,0:T(8,128)}, f32[1,128,128]{2,1,0:T(8,128)S(1)}, u32[]{:S(2)}) copy-start(f32[1,128,128]{2,1,0:T(8,128)S(1)} %get-tuple-element.51) | copy-start | bytes 196612
  114.8 4.1 %copy-start.37 = (f32[1,128,128]{2,1,0:T(8,128)}, f32[1,128,128]{2,1,0:T(8,128)S(1)}, u32[]{:S(2)}) copy-start(f32[1,128,128]{2,1,0:T(8,128)S(1)} %get-tuple-element.41) | copy-start | bytes 196612
  114.8 4.1 %copy-start.38 = (f32[1,128,128]{2,1,0:T(8,128)}, f32[1,128,128]{2,1,0:T(8,128)S(1)}, u32[]{:S(2)}) copy-start(f32[1,128,128]{2,1,0:T(8,128)S(1)} %get-tuple-element.42) | copy-start | bytes 196612
  114.8 4.1 %copy-start.39 = (f32[1,128,128]{2,1,0:T(8,128)}, f32[1,128,128]{2,1,0:T(8,128)S(1)}, u32[]{:S(2)}) copy-start(f32[1,128,128]{2,1,0:T(8,128)S(1)} %get-tuple-element.43) | copy-start | bytes 196612
  114.8 4.1 %copy-start.40 = (f32[1,128,128]{2,1,0:T(8,128)}, f32[1,128,128]{2,1,0:T(8,128)S(1)}, u32[]{:S(2)}) copy-start(f32[1,128,128]{2,1,0:T(8,128)S(1)} %get-tuple-element.44) | copy-start | bytes 196612
  114.9 4.1 %copy-start.41 = (f32[1,128,128]{2,1,0:T(8,128)}, f32[1,128,128]{2,1,0:T(8,128)S(1)}, u32[]{:S(2)}) copy-start(f32[1,128,128]{2,1,0:T(8,128)S(1)} %get-tuple-element.45) | copy-start | bytes 196612
  123.7 6.4 %copy-start.5 = (f32[3,16384]{1,0:T(4,128)S(1)}, f32[3,16384]{1,0:T(4,128)}, u32[]{:S(2)}) copy-start(f32[3,16384]{1,0:T(4,128)} %fusion.5) | copy-start | bytes 589828
  133.1 10.4 %copy-start.4 = (f32[2,3,1,128,128]{4,3,2,1,0:T(8,128)S(1)}, f32[2,3,1,128,128]{4,3,2,1,0:T(8,128)}, u32[]{:S(2)}) copy-start(f32[2,3,1,128,128]{4,3,2,1,0:T(8,128)} %param.15) | copy-start | bytes 1179652
  133.1 10.4 %copy-start.7 = (f32[128,128]{1,0:T(8,128)S(1)}, f32[128,128]{1,0:T(8,128)}, u32[]{:S(2)}) copy-start(f32[128,128]{1,0:T(8,128)} %copy-done.6) | copy-start | bytes 196612
  133.1 10.4 %copy-start.51 = (f32[2,1,128,128]{3,2,1,0:T(8,128)S(1)}, f32[2,1,128,128]{3,2,1,0:T(8,128)}, u32[]{:S(2)}) copy-start(f32[2,1,128,128]{3,2,1,0:T(8,128)} %param.14) | copy-start | bytes 393220
  140.6 152.7 %collective-permute-start.2 = (f32[10,1,128,128]{3,2,1,0:T(8,128)}, f32[10,1,128,128]{3,2,1,0:T(8,128)}, u32[]{:S(2)}, u32[]{:S(2)}) collective-permute-start(f32[10,1,128,128]{3,2,1,0:T(8,128)} %constant_dynamic-update-slice_fusion), channel_id=1, source_target_pairs={{1,0},{2,1},{3,2},{4,3},{5,4},{6,5},{7,6},{8,7},{9,8},{10,9},{11,1... | collective-permute-start | bytes 1966088 | tf_op jit(solution)/shard_map/ppermute | solution.py:16
  143.5 149.8 %collective-permute-start.3 = (f32[10,1,128,128]{3,2,1,0:T(8,128)}, f32[10,1,128,128]{3,2,1,0:T(8,128)}, u32[]{:S(2)}, u32[]{:S(2)}) collective-permute-start(f32[10,1,128,128]{3,2,1,0:T(8,128)} %constant_dynamic-update-slice_fusion), channel_id=1, source_target_pairs={{0,1},{1,2},{2,3},{3,4},{4,5},{5,6},{6,7},{7,8},{8,9},{9,10},{10,1... | collective-permute-start | bytes 1966088 | tf_op jit(solution)/shard_map/ppermute | solution.py:13
  294.5 4.6 %copy-start.12 = (f32[1,1,128,128]{3,2,1,0:T(8,128)}, f32[1,1,128,128]{3,2,1,0:T(8,128)S(1)}, u32[]{:S(2)}) copy-start(f32[1,1,128,128]{3,2,1,0:T(8,128)S(1)} %get-tuple-element.63) | copy-start | bytes 196612
  294.5 4.6 %copy-start.13 = (f32[1,1,128,128]{3,2,1,0:T(8,128)}, f32[1,1,128,128]{3,2,1,0:T(8,128)S(1)}, u32[]{:S(2)}) copy-start(f32[1,1,128,128]{3,2,1,0:T(8,128)S(1)} %get-tuple-element.87) | copy-start | bytes 196612
  294.5 4.6 %copy-start.14 = (f32[1,1,128,128]{3,2,1,0:T(8,128)}, f32[1,1,128,128]{3,2,1,0:T(8,128)S(1)}, u32[]{:S(2)}) copy-start(f32[1,1,128,128]{3,2,1,0:T(8,128)S(1)} %get-tuple-element.92) | copy-start | bytes 196612
  294.9 4.3 %copy-start.15 = (f32[1,128,128]{2,1,0:T(8,128)}, f32[1,128,128]{2,1,0:T(8,128)S(1)}, u32[]{:S(2)}) copy-start(f32[1,128,128]{2,1,0:T(8,128)S(1)} %get-tuple-element.83) | copy-start | bytes 196612
  294.9 4.3 %copy-start.16 = (f32[1,128,128]{2,1,0:T(8,128)}, f32[1,128,128]{2,1,0:T(8,128)S(1)}, u32[]{:S(2)}) copy-start(f32[1,128,128]{2,1,0:T(8,128)S(1)} %get-tuple-element.84) | copy-start | bytes 196612
  294.9 4.3 %copy-start.17 = (f32[1,128,128]{2,1,0:T(8,128)}, f32[1,128,128]{2,1,0:T(8,128)S(1)}, u32[]{:S(2)}) copy-start(f32[1,128,128]{2,1,0:T(8,128)S(1)} %get-tuple-element.100) | copy-start | bytes 196612
  (70 other events, 143.8 us)
where the time goes:
time: 318 us; the launch traced here: 312 us
  local copies, waits for them, and re-layouts  128 us (40%)
  other arithmetic  92.9 us (29%)
  blocking collectives  61.3 us (19%)
  matrix products  21.1 us (7%)
  starting transfers between devices  5.51 us (2%)
    gather x1, local copies, waits for them, and re-layouts, body(): target_rows = jnp.take(owner, patch_map)  90.5 us
    scatter-add x1, other arithmetic, body(): jax.ops.segment_sum(wall_total.reshape(-1), target_rows.reshape(-1), num_...  85.9 us
    unnamed x1, blocking collectives  61.3 us
    unnamed x218, local copies, waits for them, and re-layouts  22.2 us
    another operation x2, local copies, waits for them, and re-layouts, reverse_step(): propagated = jnp.stack(propagated)  10.9 us
    dot_general x2, matrix products, collide_adjoint(): jnp.dot(moment_table.T, relax_rates[:, None] * moments, precision=highest)  7.15 us
  transfers between devices with their start and end apart: 4, of which 0 were waited for; matrix products, arithmetic and copies ran while one was open for 58% of the time, Pallas kernels for 0%

commit v1 on v0

v1 whole, which is shorter than its diff:
```python
import functools

import jax
import jax.numpy as jnp
import numpy as np
from jax import lax
from jax.experimental import pallas as pl
from jax.experimental.pallas import tpu as pltpu
from jax.sharding import PartitionSpec as P

MESH = pl.DeviceIdType.MESH
RISING = (1, 7, 9, 11, 13)
FALLING = (2, 8, 10, 12, 14)
OPPOSITE = (0, 2, 1, 4, 3, 6, 5, 8, 7, 10, 9, 12, 11, 14, 13, 16, 15, 18, 17)
VELOCITIES = (
    (0, 0, 0),
    (1, 0, 0),
    (-1, 0, 0),
    (0, 1, 0),
    (0, -1, 0),
    (0, 0, 1),
    (0, 0, -1),
    (1, 1, 0),
    (-1, -1, 0),
    (1, -1, 0),
    (-1, 1, 0),
    (1, 0, 1),
    (-1, 0, -1),
    (1, 0, -1),
    (-1, 0, 1),
    (0, 1, 1),
    (0, -1, -1),
    (0, 1, -1),
    (0, -1, 1),
)
PAD = 8
ROWS = 8


def moment_table():
    lattice = np.asarray(VELOCITIES, np.float32)
    x, y, z = lattice[:, 0], lattice[:, 1], lattice[:, 2]
    monomials = [np.ones((19,), np.float32), x, y, z, x * y, x * z, y * z, x * x, y * y, z * z]
    monomials += [x * y * y, x * z * z, y * x * x, z * x * x, y * z * z, z * y * y]
    monomials += [x * x * y * y, x * x * z * z, y * y * z * z]
    basis = []
    for vector in monomials:
        for sweep in range(2):
            for earlier in basis:
                vector = vector - np.sum(vector * earlier) * earlier
        basis.append(vector / np.sqrt(np.sum(vector * vector)))
    return np.stack(basis)


TABLE = moment_table()
EVEN_AT = (0, 1, 3, 5, 7, 11, 15)
EVEN_ROWS = (7, 8, 9, 16, 17, 18)
ODD_AT = ((1, 7, 11), (3, 7, 15), (5, 11, 15))
ODD_ROWS = ((10, 11), (12, 14), (13, 15))
MIXED = ((4, 7), (5, 11), (6, 15))


def coefficients(relax_ref):
    def block(at, rows):
        rates = [relax_ref[row] for row in rows]
        out = {}
        for a in range(len(at)):
            for b in range(a, len(at)):
                total = None
                for row, rate in zip(rows, rates):
                    factor = float(TABLE[row, at[a]]) * float(TABLE[row, at[b]])
                    if abs(factor) < 1e-6:
                        continue
                    term = rate * np.float32(factor)
                    total = term if total is None else total + term
                out[a, b] = out[b, a] = total
        return out

    even = block(EVEN_AT, EVEN_ROWS)
    odd = [block(at, rows) for at, rows in zip(ODD_AT, ODD_ROWS)]
    mixed = [relax_ref[row] * np.float32(float(TABLE[row, at]) ** 2) for row, at in MIXED]
    return even, odd, mixed


def apply(block, values):
    result = []
    for a in range(len(values)):
        total = None
        for b, value in enumerate(values):
            if block[a, b] is None:
                continue
            term = block[a, b] * value
            total = term if total is None else total + term
        result.append(total)
    return result


def classes(p):
    even = [p[0], p[1] + p[2], p[3] + p[4], p[5] + p[6]]
    single = [p[1] - p[2], p[3] - p[4], p[5] - p[6]]
    mixed, firsts, seconds = [], [], []
    for base in (7, 11, 15):
        a, b = p[base] + p[base + 1], p[base + 2] + p[base + 3]
        c, d = p[base] - p[base + 1], p[base + 2] - p[base + 3]
        even.append(a + b)
        mixed.append(a - b)
        firsts.append(c + d)
        seconds.append(c - d)
    odd = [
        [single[0], firsts[0], firsts[1]],
        [single[1], seconds[0], firsts[2]],
        [single[2], seconds[1], seconds[2]],
    ]
    return even, odd, mixed


def quadratic(diagonal, mixed, u):
    xx, yy, zz = diagonal
    xy, xz, yz = mixed
    return (
        u[0] * xx + u[1] * xy + u[2] * xz,
        u[0] * xy + u[1] * yy + u[2] * yz,
        u[0] * xz + u[1] * yz + u[2] * zz,
    )


def collide(p, u, fluid, coefs):
    even_block, odd_block, mixed_block = coefs
    even, odd, mixed = classes(p)
    ge = apply(even_block, even)
    go = [apply(block, values) for block, values in zip(odd_block, odd)]
    gm = [scale * value for scale, value in zip(mixed_block, mixed)]
    w0, w1, w2 = np.float32(1 / 3), np.float32(2 / 18), np.float32(4 / 36)
    axes = [w1 * value for value in ge[1:4]]
    planes = [w2 * value for value in ge[4:7]]
    diagonal = (
        axes[0] + (planes[0] + planes[1]),
        axes[1] + (planes[0] + planes[2]),
        axes[2] + (planes[1] + planes[2]),
    )
    total = w0 * ge[0] + (axes[0] + axes[1] + axes[2]) + (planes[0] + planes[1] + planes[2])
    first = [w1 * value[0] + w2 * (value[1] + value[2]) for value in go]
    cross = [w2 * value for value in gm]
    bent = quadratic(diagonal, cross, u)
    speed_sq = u[0] * u[0] + u[1] * u[1] + u[2] * u[2]
    s0 = total * (1.0 + 1.5 * speed_sq) - 4.5 * (u[0] * bent[0] + u[1] * bent[1] + u[2] * bent[2])
    s = [3.0 * (first[i] + 3.0 * bent[i] - u[i] * total) for i in range(3)]
    he = [s0 - value for value in ge]
    ho = [[s[i] - value for value in go[i]] for i in range(3)]
    out = [None] * 19
    out[0] = p[0] + he[0]
    for i in range(3):
        out[1 + 2 * i] = p[1 + 2 * i] + (he[1 + i] + ho[i][0])
        out[2 + 2 * i] = p[2 + 2 * i] + (he[1 + i] - ho[i][0])
    pairs = ((ho[0][1], ho[1][1]), (ho[0][2], ho[2][1]), (ho[1][2], ho[2][2]))
    for i, (left, right) in enumerate(pairs):
        base = 7 + 4 * i
        e, f = he[4 + i] - gm[i], he[4 + i] + gm[i]
        x, y = left + right, left - right
        out[base] = p[base] + (e + x)
        out[base + 1] = p[base + 1] + (e - x)
        out[base + 2] = p[base + 2] + (f + y)
        out[base + 3] = p[base + 3] + (f - y)
    return [jnp.where(fluid, value, 0.0) for value in out]


def wall_value(x, rho, u, fluid):
    even, odd, mixed = classes(x)
    total = sum(even[1:], even[0])
    diagonal = (
        even[1] + (even[4] + even[5]),
        even[2] + (even[4] + even[6]),
        even[3] + (even[5] + even[6]),
    )
    first = [value[0] + (value[1] + value[2]) for value in odd]
    bent = quadratic(diagonal, mixed, u)
    speed_sq = u[0] * u[0] + u[1] * u[1] + u[2] * u[2]
    linear = [3.0 * first[i] + 4.5 * bent[i] for i in range(3)]
    value = total * (1.0 - 1.5 * speed_sq) + (
        u[0] * linear[0] + u[1] * linear[1] + u[2] * linear[2]
    )
    return jnp.where(fluid, rho * value, 0.0)


def split3(value):
    one = value.astype(jnp.bfloat16)
    rest = value - one.astype(jnp.float32)
    two = rest.astype(jnp.bfloat16)
    three = (rest - two.astype(jnp.float32)).astype(jnp.bfloat16)
    return [part.astype(jnp.float32) for part in (one, two, three)]


def one_hot_sums(index, value, low_bits, highs):
    high = lax.shift_right_logical(index, low_bits)
    low = lax.bitwise_and(index, (1 << low_bits) - 1)
    parts = split3(value)
    high_iota = lax.broadcasted_iota(jnp.int32, (highs, 128), 0)
    low_iota = lax.broadcasted_iota(jnp.int32, (128, 128), 0)
    lefts, rights = [], []
    for row in range(ROWS):
        hit = high_iota == high[row : row + 1, :]
        left = [jnp.where(hit, part[row : row + 1, :], 0.0) for part in parts]
        lefts.append(jnp.concatenate(left, axis=0).astype(jnp.bfloat16))
        right = jnp.where(low_iota == low[row : row + 1, :], 1.0, 0.0)
        rights.append(right.astype(jnp.bfloat16))
    return lax.dot_general(
        jnp.concatenate(lefts, axis=1),
        jnp.concatenate(rights, axis=1),
        (((1,), (1,)), ((), ())),
        preferred_element_type=jnp.float32,
    )


def kernel(
    n,
    low_bits,
    relax_ref,
    adjoint_ref,
    density_ref,
    velocity_ref,
    links_ref,
    patch_ref,
    owner_ref,
    out_ref,
    gradient_ref,
    first,
    second,
    rims_one,
    rims_two,
    rho,
    flow,
    bits,
    patch,
    owner,
    wall,
    sums,
    outgoing,
    incoming,
    local_sem,
    send_one,
    recv_one,
    send_two,
    recv_two,
    send_sum,
    recv_sum,
):
    me = lax.axis_index("span")
    above, below = lax.rem(me + 1, n), lax.rem(me + n - 1, n)
    ny = wall.shape[0]
    chunks = ny // ROWS

    def other(d):
        return lax.rem(me + d, n)

    loads = [
        pltpu.make_async_copy(source, target, local_sem.at[i])
        for i, (source, target) in enumerate(
            (
                (adjoint_ref.at[:, 0], first.at[:, pl.ds(PAD, ny), :]),
                (links_ref.at[:, 0], bits),
                (velocity_ref.at[:, :, 0], flow),
                (density_ref.at[:, 0], rho),
                (patch_ref.at[0], patch),
                (owner_ref, owner),
            )
        )
    ]
    for load in loads:
        load.start()

    barrier = pltpu.get_barrier_semaphore()

    def greet(d, carry):
        pl.semaphore_signal(barrier, inc=1, device_id={"span": other(d)}, device_id_type=MESH)
        return carry

    lax.fori_loop(1, n, greet, 0)
    for buffer in (first, second, rims_one, rims_two):
        blank = jnp.zeros((buffer.shape[0], PAD, buffer.shape[2]), jnp.float32)
        buffer[:, 0:PAD, :] = blank
        buffer[:, PAD + ny : PAD + ny + PAD, :] = blank
    pl.semaphore_wait(barrier, n - 1)

    def exchange(plane_of, rims, send_sem, recv_sem):
        copies = []
        for k in range(5):
            for slot, direction, target in ((k, RISING[k], below), (5 + k, FALLING[k], above)):
                copies.append(
                    pltpu.make_async_remote_copy(
                        src_ref=plane_of(direction),
                        dst_ref=rims.at[slot, pl.ds(PAD, ny), :],
                        send_sem=send_sem.at[slot],
                        recv_sem=recv_sem.at[slot],
                        device_id={"span": target},
                        device_id_type=MESH,
                    )
                )
        for copy in copies:
            copy.start()
        return copies

    copies_one = exchange(lambda j: adjoint_ref.at[j, 0], rims_one, send_one, recv_one)
    coefs = coefficients(relax_ref)
    for load in loads:
        load.wait()

    def masks(rows):
        low, high = bits[0, rows, :], bits[1, rows, :]
        return [
            lax.bitwise_and(low if j < 10 else high, 1 << (j % 10)) != 0 for j in range(19)
        ]

    def walls(level, populations, add):
        def step(i, carry):
            start = pl.multiple_of(i * ROWS, ROWS)
            rows = pl.ds(start, ROWS)
            inner = pl.ds(pl.multiple_of(start + PAD, ROWS), ROWS)
            linked = masks(rows)
            u = [flow[level, axis, rows, :] for axis in range(3)]
            x = [
                jnp.where(linked[j], populations[OPPOSITE[j], inner, :], 0.0) for j in range(19)
            ]
            value = wall_value(x, rho[level, rows, :], u, jnp.logical_not(linked[0]))
            wall[rows, :] = wall[rows, :] + value if add else value
            return carry

        lax.fori_loop(0, chunks, step, 0)

    def collisions(level, populations, rims, store):
        def step(i, carry):
            start = pl.multiple_of(i * ROWS, ROWS)
            rows = pl.ds(start, ROWS)
            inner = pl.ds(pl.multiple_of(start + PAD, ROWS), ROWS)
            linked = masks(rows)
            u = [flow[level, axis, rows, :] for axis in range(3)]
            p = []
            for j, (step_x, step_y, step_z) in enumerate(VELOCITIES):
                shifted = inner if step_y == 0 else pl.ds(start + (PAD + step_y), ROWS)
                if step_x == 1:
                    upstream = rims[RISING.index(j), shifted, :]
                elif step_x == -1:
                    upstream = rims[5 + FALLING.index(j), shifted, :]
                else:
                    upstream = populations[j, shifted, :]
                if step_z != 0:
                    upstream = pltpu.roll(upstream, (-step_z) % upstream.shape[1], 1)
                p.append(jnp.where(linked[j], populations[OPPOSITE[j], inner, :], upstream))
            for j, value in enumerate(collide(p, u, jnp.logical_not(linked[0]), coefs)):
                store(j, rows, inner, value)
            return carry

        lax.fori_loop(0, chunks, step, 0)

    walls(1, first, False)
    for copy in copies_one:
        copy.wait_recv()

    def store_second(j, rows, inner, value):
        second[j, inner, :] = value

    collisions(1, first, rims_one, store_second)
    copies_two = exchange(lambda j: second.at[j, pl.ds(PAD, ny), :], rims_two, send_two, recv_two)

    walls(0, second, True)

    def by_patch(i, total):
        rows = pl.ds(pl.multiple_of(i * ROWS, ROWS), ROWS)
        return total + one_hot_sums(patch[rows, :], wall[rows, :], 7, owner.shape[0])

    highs = owner.shape[0]
    total = lax.fori_loop(0, chunks, by_patch, jnp.zeros((3 * highs, 128), jnp.float32))
    sums[...] = total[:highs] + (total[highs : 2 * highs] + total[2 * highs :])

    targets = outgoing.shape[0] * outgoing.shape[1]

    def by_owner(i, total):
        rows = pl.ds(pl.multiple_of(i * ROWS, ROWS), ROWS)
        return total + one_hot_sums(owner[rows, :], sums[rows, :], low_bits, targets)

    total = lax.fori_loop(
        0, highs // ROWS, by_owner, jnp.zeros((3 * targets, 128), jnp.float32)
    )
    placed = total[:targets] + (total[targets : 2 * targets] + total[2 * targets :])
    per = outgoing.shape[1]
    for i in range(n):
        outgoing[i] = placed[i * per : (i + 1) * per]

    def sum_copy(d, source):
        return pltpu.make_async_remote_copy(
            src_ref=outgoing.at[other(d)],
            dst_ref=incoming.at[source],
            send_sem=send_sum.at[d],
            recv_sem=recv_sum.at[source],
            device_id={"span": other(d)},
            device_id_type=MESH,
        )

    def send(d, carry):
        sum_copy(d, me).start()
        return carry

    lax.fori_loop(1, n, send, 0)

    for copy in copies_two:
        copy.wait_recv()

    def store_out(j, rows, inner, value):
        out_ref[j, 0, rows, :] = value

    collisions(0, second, rims_two, store_out)

    def collect(d, total):
        source = other(n - d)
        sum_copy(d, source).wait_recv()
        return total + incoming[source]

    gradient_ref[...] = lax.fori_loop(1, n, collect, outgoing[me])

    def sent(d, carry):
        sum_copy(d, me).wait_send()
        return carry

    lax.fori_loop(1, n, sent, 0)
    for copy in copies_one + copies_two:
        copy.wait_send()


def body(n, adjoint_in, density, velocity, links, patch_map, owner, relax):
    _, planes, ny, nz = adjoint_in.shape
    assert planes == 1 and nz == 128 and ny % ROWS == 0
    rows = owner.shape[0] // n
    low = min(128, rows)
    per = rows // low
    highs = owner.shape[0] // 128
    padded = ny + 2 * PAD
    hbm = pl.BlockSpec(memory_space=pl.ANY)
    vmem = pl.BlockSpec(memory_space=pltpu.VMEM)
    levels = density.shape[0]
    adjoint, gradient = pl.pallas_call(
        functools.partial(kernel, n, low.bit_length() - 1),
        out_shape=(
            jax.ShapeDtypeStruct(adjoint_in.shape, jnp.float32),
            jax.ShapeDtypeStruct((per, 128), jnp.float32),
        ),
        in_specs=[pl.BlockSpec(memory_space=pltpu.SMEM)] + [hbm] * 6,
        out_specs=(vmem, vmem),
        scratch_shapes=[
            pltpu.VMEM((19, padded, nz), jnp.float32),
            pltpu.VMEM((19, padded, nz), jnp.float32),
            pltpu.VMEM((10, padded, nz), jnp.float32),
            pltpu.VMEM((10, padded, nz), jnp.float32),
            pltpu.VMEM((levels, ny, nz), jnp.float32),
            pltpu.VMEM((levels, 3, ny, nz), jnp.float32),
            pltpu.VMEM((2, ny, nz), jnp.int32),
            pltpu.VMEM((ny, nz), jnp.int32),
            pltpu.VMEM((highs, 128), jnp.int32),
            pltpu.VMEM((ny, nz), jnp.float32),
            pltpu.VMEM((highs, 128), jnp.float32),
            pltpu.VMEM((n, per, 128), jnp.float32),
            pltpu.VMEM((n, per, 128), jnp.float32),
            pltpu.SemaphoreType.DMA((6,)),
            pltpu.SemaphoreType.DMA((10,)),
            pltpu.SemaphoreType.DMA((10,)),
            pltpu.SemaphoreType.DMA((10,)),
            pltpu.SemaphoreType.DMA((10,)),
            pltpu.SemaphoreType.DMA((n,)),
            pltpu.SemaphoreType.DMA((n,)),
        ],
        compiler_params=pltpu.CompilerParams(
            collective_id=0, has_side_effects=True, vmem_limit_bytes=32 * 1024 * 1024
        ),
        cost_estimate=pl.CostEstimate(
            flops=40_000_000, bytes_accessed=4_000_000, transcendentals=0
        ),
    )(relax, adjoint_in, density, velocity, links, patch_map, owner.reshape(highs, 128))
    return adjoint, gradient[:, :low].reshape(rows)


def solution(mesh):
    in_specs = (
        P("case", "span", None, None),
        P("case", "span", None, None),
        P("case", None, "span", None, None),
        P(None, ("case", "span"), None, None),
        P(("case", "span"), None, None),
        P(),
        P("case"),
    )
    out_specs = (P("case", "span", None, None), P(("case", "span")))
    return jax.shard_map(
        functools.partial(body, mesh.shape["span"]),
        mesh=mesh,
        in_specs=in_specs,
        out_specs=out_specs,
        check_vma=False,
    )
```

time: 318 us -> 38 us (0.12); the launches traced: 312 us -> 37.7 us
  local copies, waits for them, and re-layouts: 128 us -> 7.9 us
  other arithmetic: 92.9 us -> 0 us
  blocking collectives: 61.3 us -> 0 us
  Pallas kernels: 0 us -> 29.1 us
  matrix products: 21.1 us -> 0 us
  starting transfers between devices: 5.51 us -> 0 us
    gather x1 -> x0, local copies, waits for them, and re-layouts: 90.5 us -> none  [body(): target_rows = jnp.take(owner, patch_map)]
    scatter-add x1 -> x0, other arithmetic: 85.9 us -> none  [body(): jax.ops.segment_sum(wall_total.reshape(-1), target_rows.reshape(-1), num_...]
    unnamed x1 -> x0, blocking collectives: 61.3 us -> none
    pallas_call x0 -> x1, Pallas kernels: none -> 29.1 us  [body(): pl.pallas_call(functools.partial(kernel, n, low.bit_length() - 1), out_sh...]
    dot_general x8 -> x0, matrix products: 21.1 us -> none  [the longest x2 7.15 us: collide_adjoint(): jnp.dot(moment_table.T, relax_rates[:, None] * moments, precision=highest)]
    unnamed x218 -> x16, local copies, waits for them, and re-layouts: 22.2 us -> 7.9 us
    another operation x4 -> x0, local copies, waits for them, and re-layouts: 13 us -> none  [the longest x2 10.9 us: reverse_step(): propagated = jnp.stack(propagated)]
    ppermute x4 -> x0, starting transfers between devices: 5.51 us -> none  [the longest x2 2.93 us: padded_2(): lax.ppermute(lax.slice_in_dim(block, 0, width, axis=dim), axis, backward)]
  transfers between devices with their start and end apart: 4 -> 0, of which waited for: 0 -> 0; matrix products, arithmetic and copies ran while one was open for 58% -> 0% of each run, Pallas kernels for 0% -> 0%
where the time goes in v1:
time: 38 us; the launch traced here: 37.7 us
  Pallas kernels  29.1 us (77%)
  local copies, waits for them, and re-layouts  7.9 us (21%)
  between operations  0.66 us (2%)
    pallas_call x1, Pallas kernels, body(): pl.pallas_call(functools.partial(kernel, n, low.bit_length() - 1), out_sh...  29.1 us
    unnamed x16, local copies, waits for them, and re-layouts  7.9 us

profile of v1, /device:TPU:1, one launch (start us, length us, event | category | flops | bytes accessed | tf_op | source)
XLA Modules:
  0.0 37.7 jit_solution(7501568162966856911)
XLA Ops:
  0.6 0.0 copy-start
  0.6 1.3 %copy-done = f32[19,1,128,128]{3,2,1,0:T(8,128)S(1)} copy-done((f32[19,1,128,128]{3,2,1,0:T(8,128)S(1)}, f32[19,1,128,128]{3,2,1,0:T(8,128)}, u32[]{:S(2)}) %copy-start) | copy-done | bytes 1245208
  1.9 0.0 copy-start.1
  1.9 1.0 %copy-done.1 = f32[2,3,1,128,128]{4,3,2,1,0:T(8,128)S(1)} copy-done((f32[2,3,1,128,128]{4,3,2,1,0:T(8,128)S(1)}, f32[2,3,1,128,128]{4,3,2,1,0:T(8,128)}, u32[]{:S(2)}) %copy-start.1) | copy-done | bytes 393240
  2.9 0.0 copy-start.2
  2.9 0.9 %copy-done.2 = f32[2,1,128,128]{3,2,1,0:T(8,128)S(1)} copy-done((f32[2,1,128,128]{3,2,1,0:T(8,128)S(1)}, f32[2,1,128,128]{3,2,1,0:T(8,128)}, u32[]{:S(2)}) %copy-start.2) | copy-done | bytes 131096
  3.8 0.0 copy-start.3
  3.8 0.9 %copy-done.3 = s32[2,1,128,128]{3,2,1,0:T(8,128)S(1)} copy-done((s32[2,1,128,128]{3,2,1,0:T(8,128)S(1)}, s32[2,1,128,128]{3,2,1,0:T(8,128)}, u32[]{:S(2)}) %copy-start.3) | copy-done | bytes 131096
  4.7 0.0 copy-start.4
  4.7 0.8 %copy-done.4 = s32[1,128,128]{2,1,0:T(8,128)S(1)} copy-done((s32[1,128,128]{2,1,0:T(8,128)S(1)}, s32[1,128,128]{2,1,0:T(8,128)}, u32[]{:S(2)}) %copy-start.4) | copy-done | bytes 65560
  5.6 0.0 copy-start.5
  5.6 0.7 %copy-done.5 = s32[4096]{0:T(1024)S(1)} copy-done((s32[4096]{0:T(1024)S(1)}, s32[4096]{0:T(1024)}, u32[]{:S(2)}) %copy-start.5) | copy-done | bytes 16408
  6.3 0.0 copy-start.6
  6.3 0.7 %copy-done.6 = f32[19]{0:T(128)S(1)} copy-done((f32[19]{0:T(128)S(1)}, f32[19]{0:T(128)}, u32[]{:S(2)}) %copy-start.6) | copy-done | bytes 100
  6.9 29.1 %shard_map.86 = (f32[19,1,128,128]{3,2,1,0:T(8,128)S(1)}, f32[2,128]{1,0:T(2,128)S(1)}) custom-call(f32[19]{0:T(128)S(1)} %copy-done.6, f32[19,1,128,128]{3,2,1,0:T(8,128)S(1)} %copy-done, f32[2,1,128,128]{3,2,1,0:T(8,128)S(1)} %copy-done.2, f32[2,3,1,128,128]{4,3,2,1,0:T(8,128)S(1)} %copy-done.1, s32[2,1,128,128]{3,2,1,0:T(8,128)S(1)} %copy-done.3, ...), custom_call_target="tpu_custom_call" | custom-call | flops 40000000 | bytes 4000000 | tf_op jit(solution)/shard_map/pallas_call | solution.py:439
  36.1 1.0 %copy.11 = f32[19,1,128,128]{3,2,1,0:T(8,128)} copy(f32[19,1,128,128]{3,2,1,0:T(8,128)S(1)} %get-tuple-element.8) | data formatting | bytes 2490368
  37.1 0.6 %copy.12 = f32[256]{0:T(256)} copy(f32[256]{0:T(256)S(1)} %bitcast.3) | data formatting | bytes 2048
Async XLA Ops:
  0.6 1.3 %copy-start = (f32[19,1,128,128]{3,2,1,0:T(8,128)S(1)}, f32[19,1,128,128]{3,2,1,0:T(8,128)}, u32[]{:S(2)}) copy-start(f32[19,1,128,128]{3,2,1,0:T(8,128)} %adjoint_ref.1) | copy-start | bytes 3735556
  1.9 1.0 %copy-start.1 = (f32[2,3,1,128,128]{4,3,2,1,0:T(8,128)S(1)}, f32[2,3,1,128,128]{4,3,2,1,0:T(8,128)}, u32[]{:S(2)}) copy-start(f32[2,3,1,128,128]{4,3,2,1,0:T(8,128)} %velocity_ref.1) | copy-start | bytes 1179652
  2.9 0.9 %copy-start.2 = (f32[2,1,128,128]{3,2,1,0:T(8,128)S(1)}, f32[2,1,128,128]{3,2,1,0:T(8,128)}, u32[]{:S(2)}) copy-start(f32[2,1,128,128]{3,2,1,0:T(8,128)} %density_ref.1) | copy-start | bytes 393220
  3.8 0.9 %copy-start.3 = (s32[2,1,128,128]{3,2,1,0:T(8,128)S(1)}, s32[2,1,128,128]{3,2,1,0:T(8,128)}, u32[]{:S(2)}) copy-start(s32[2,1,128,128]{3,2,1,0:T(8,128)} %links_ref.1) | copy-start | bytes 393220
  4.7 0.8 %copy-start.4 = (s32[1,128,128]{2,1,0:T(8,128)S(1)}, s32[1,128,128]{2,1,0:T(8,128)}, u32[]{:S(2)}) copy-start(s32[1,128,128]{2,1,0:T(8,128)} %patch_ref.1) | copy-start | bytes 196612
  5.6 0.7 %copy-start.5 = (s32[4096]{0:T(1024)S(1)}, s32[4096]{0:T(1024)}, u32[]{:S(2)}) copy-start(s32[4096]{0:T(1024)} %param.12) | copy-start | bytes 49156
  6.3 0.7 %copy-start.6 = (f32[19]{0:T(128)S(1)}, f32[19]{0:T(128)}, u32[]{:S(2)}) copy-start(f32[19]{0:T(128)} %relax_ref.1) | copy-start | bytes 232

commit v2 on v1

--- a/solution.py
+++ b/solution.py
@@ -35,6 +35,9 @@
 )
 PAD = 8
 ROWS = 8
+PIECES = 1
+ORDER = RISING + FALLING + (0, 3, 4, 5, 6, 15, 16, 17, 18)
+PLACE = tuple(ORDER.index(j) for j in range(19))
 
 
 def moment_table():
@@ -214,7 +217,7 @@
 def kernel(
     n,
     low_bits,
-    relax_ref,
+    relax_hbm,
     adjoint_ref,
     density_ref,
     velocity_ref,
@@ -232,6 +235,7 @@
     bits,
     patch,
     owner,
+    relax_ref,
     wall,
     sums,
     outgoing,
@@ -243,6 +247,9 @@
     recv_two,
     send_sum,
     recv_sum,
+    result,
+    out_sem,
+    met,
 ):
     me = lax.axis_index("span")
     above, below = lax.rem(me + 1, n), lax.rem(me + n - 1, n)
@@ -262,6 +269,7 @@
                 (density_ref.at[:, 0], rho),
                 (patch_ref.at[0], patch),
                 (owner_ref, owner),
+                (relax_hbm, relax_ref),
             )
         )
     ]
@@ -270,39 +278,68 @@
 
     barrier = pltpu.get_barrier_semaphore()
 
-    def greet(d, carry):
-        pl.semaphore_signal(barrier, inc=1, device_id={"span": other(d)}, device_id_type=MESH)
-        return carry
-
-    lax.fori_loop(1, n, greet, 0)
+    neighbours = (above, below) if n > 2 else (above,)
+    for device in neighbours:
+        pl.semaphore_signal(barrier, inc=1, device_id={"span": device}, device_id_type=MESH)
     for buffer in (first, second, rims_one, rims_two):
         blank = jnp.zeros((buffer.shape[0], PAD, buffer.shape[2]), jnp.float32)
         buffer[:, 0:PAD, :] = blank
         buffer[:, PAD + ny : PAD + ny + PAD, :] = blank
-    pl.semaphore_wait(barrier, n - 1)
-
-    def exchange(plane_of, rims, send_sem, recv_sem):
+    pl.semaphore_wait(barrier, len(neighbours))
+
+    pieces = PIECES
+    length = ny // pieces
+    ends_one = [length * (i + 1) for i in range(pieces)]
+    ends_two = [end - ROWS for end in ends_one[:-1]] + [ny]
+    ends_out = [end - ROWS for end in ends_two[:-1]] + [ny]
+
+    def send_rims(sources, rims, sems, start, end):
         copies = []
-        for k in range(5):
-            for slot, direction, target in ((k, RISING[k], below), (5 + k, FALLING[k], above)):
-                copies.append(
-                    pltpu.make_async_remote_copy(
-                        src_ref=plane_of(direction),
-                        dst_ref=rims.at[slot, pl.ds(PAD, ny), :],
-                        send_sem=send_sem.at[slot],
-                        recv_sem=recv_sem.at[slot],
-                        device_id={"span": target},
-                        device_id_type=MESH,
-                    )
+        for i, (slots, source, target) in enumerate(sources(start, end)):
+            copies.append(
+                pltpu.make_async_remote_copy(
+                    src_ref=source,
+                    dst_ref=rims.at[slots, pl.ds(PAD + start, end - start), :],
+                    send_sem=sems[0].at[i],
+                    recv_sem=sems[1].at[i],
+                    device_id={"span": target},
+                    device_id_type=MESH,
                 )
+            )
         for copy in copies:
             copy.start()
         return copies
 
-    copies_one = exchange(lambda j: adjoint_ref.at[j, 0], rims_one, send_one, recv_one)
-    coefs = coefficients(relax_ref)
+    def sources_one(start, end):
+        rows = pl.ds(start, end - start)
+        for k in range(5):
+            yield k, adjoint_ref.at[RISING[k], 0, rows, :], below
+            yield 5 + k, adjoint_ref.at[FALLING[k], 0, rows, :], above
+
+    def sources_two(start, end):
+        rows = pl.ds(PAD + start, end - start)
+        yield pl.ds(0, 5), second.at[pl.ds(0, 5), rows, :], below
+        yield pl.ds(5, 5), second.at[pl.ds(5, 5), rows, :], above
+
+    def meet(i):
+        far = 1 << i
+        for side, device in enumerate((other(far), other(n - far))):
+            pl.semaphore_signal(
+                met.at[i, side], inc=1, device_id={"span": device}, device_id_type=MESH
+            )
+
+    def met_all(i):
+        for side in range(2):
+            pl.semaphore_wait(met.at[i, side], 1)
+
+    copies_one = []
+    for i, end in enumerate(ends_one):
+        sems = (send_one.at[i], recv_one.at[i])
+        copies_one.append(send_rims(sources_one, rims_one, sems, end - length, end))
+    meet(0)
     for load in loads:
         load.wait()
+    coefs = coefficients(relax_ref)
 
     def masks(rows):
         low, high = bits[0, rows, :], bits[1, rows, :]
@@ -310,7 +347,7 @@
             lax.bitwise_and(low if j < 10 else high, 1 << (j % 10)) != 0 for j in range(19)
         ]
 
-    def walls(level, populations, add):
+    def walls(level, populations, place, add):
         def step(i, carry):
             start = pl.multiple_of(i * ROWS, ROWS)
             rows = pl.ds(start, ROWS)
@@ -318,7 +355,7 @@
             linked = masks(rows)
             u = [flow[level, axis, rows, :] for axis in range(3)]
             x = [
-                jnp.where(linked[j], populations[OPPOSITE[j], inner, :], 0.0) for j in range(19)
+                jnp.where(linked[j], populations[place[OPPOSITE[j]], inner, :], 0.0) for j in range(19)
             ]
             value = wall_value(x, rho[level, rows, :], u, jnp.logical_not(linked[0]))
             wall[rows, :] = wall[rows, :] + value if add else value
@@ -326,7 +363,7 @@
 
         lax.fori_loop(0, chunks, step, 0)
 
-    def collisions(level, populations, rims, store):
+    def collisions(level, populations, place, rims, store, begin, end):
         def step(i, carry):
             start = pl.multiple_of(i * ROWS, ROWS)
             rows = pl.ds(start, ROWS)
@@ -341,27 +378,35 @@
                 elif step_x == -1:
                     upstream = rims[5 + FALLING.index(j), shifted, :]
                 else:
-                    upstream = populations[j, shifted, :]
+                    upstream = populations[place[j], shifted, :]
                 if step_z != 0:
                     upstream = pltpu.roll(upstream, (-step_z) % upstream.shape[1], 1)
-                p.append(jnp.where(linked[j], populations[OPPOSITE[j], inner, :], upstream))
+                p.append(jnp.where(linked[j], populations[place[OPPOSITE[j]], inner, :], upstream))
             for j, value in enumerate(collide(p, u, jnp.logical_not(linked[0]), coefs)):
                 store(j, rows, inner, value)
             return carry
 
-        lax.fori_loop(0, chunks, step, 0)
-
-    walls(1, first, False)
-    for copy in copies_one:
-        copy.wait_recv()
+        lax.fori_loop(begin // ROWS, end // ROWS, step, 0)
 
     def store_second(j, rows, inner, value):
-        second[j, inner, :] = value
-
-    collisions(1, first, rims_one, store_second)
-    copies_two = exchange(lambda j: second.at[j, pl.ds(PAD, ny), :], rims_two, send_two, recv_two)
-
-    walls(0, second, True)
+        second[PLACE[j], inner, :] = value
+
+    walls(1, first, range(19), False)
+    rounds = met.shape[0]
+    for i in range(rounds):
+        met_all(i)
+        if i + 1 < rounds:
+            meet(i + 1)
+    copies_two = []
+    for i, end in enumerate(ends_two):
+        for copy in copies_one[i]:
+            copy.wait_recv()
+        start = ends_two[i - 1] if i else 0
+        collisions(1, first, range(19), rims_one, store_second, start, end)
+        sems = (send_two.at[i], recv_two.at[i])
+        copies_two.append(send_rims(sources_two, rims_two, sems, start, end))
+
+    walls(0, second, PLACE, True)
 
     def by_patch(i, total):
         rows = pl.ds(pl.multiple_of(i * ROWS, ROWS), ROWS)
@@ -401,13 +446,22 @@
 
     lax.fori_loop(1, n, send, 0)
 
-    for copy in copies_two:
-        copy.wait_recv()
-
     def store_out(j, rows, inner, value):
-        out_ref[j, 0, rows, :] = value
-
-    collisions(0, second, rims_two, store_out)
+        result[j, 0, rows, :] = value
+
+    out_copies = []
+    for i, end in enumerate(ends_out):
+        for copy in copies_two[i]:
+            copy.wait_recv()
+        start = ends_out[i - 1] if i else 0
+        collisions(0, second, PLACE, rims_two, store_out, start, end)
+        rows = pl.ds(start, end - start)
+        out_copies.append(
+            pltpu.make_async_copy(
+                result.at[:, :, rows, :], out_ref.at[:, :, rows, :], out_sem.at[i]
+            )
+        )
+        out_copies[-1].start()
 
     def collect(d, total):
         source = other(n - d)
@@ -421,8 +475,11 @@
         return carry
 
     lax.fori_loop(1, n, sent, 0)
-    for copy in copies_one + copies_two:
-        copy.wait_send()
+    for copies in copies_one + copies_two:
+        for copy in copies:
+            copy.wait_send()
+    for copy in out_copies:
+        copy.wait()
 
 
 def body(n, adjoint_in, density, velocity, links, patch_map, owner, relax):
@@ -433,17 +490,18 @@
     per = rows // low
     highs = owner.shape[0] // 128
     padded = ny + 2 * PAD
-    hbm = pl.BlockSpec(memory_space=pl.ANY)
+    hbm = pl.BlockSpec(memory_space=pltpu.HBM)
     vmem = pl.BlockSpec(memory_space=pltpu.VMEM)
     levels = density.shape[0]
+    rounds = max(1, (n // 2 - 1).bit_length())
     adjoint, gradient = pl.pallas_call(
         functools.partial(kernel, n, low.bit_length() - 1),
         out_shape=(
             jax.ShapeDtypeStruct(adjoint_in.shape, jnp.float32),
             jax.ShapeDtypeStruct((per, 128), jnp.float32),
         ),
-        in_specs=[pl.BlockSpec(memory_space=pltpu.SMEM)] + [hbm] * 6,
-        out_specs=(vmem, vmem),
+        in_specs=[hbm] * 7,
+        out_specs=(hbm, vmem),
         scratch_shapes=[
             pltpu.VMEM((19, padded, nz), jnp.float32),
             pltpu.VMEM((19, padded, nz), jnp.float32),
@@ -454,20 +512,24 @@
             pltpu.VMEM((2, ny, nz), jnp.int32),
             pltpu.VMEM((ny, nz), jnp.int32),
             pltpu.VMEM((highs, 128), jnp.int32),
+            pltpu.SMEM(relax.shape, jnp.float32),
             pltpu.VMEM((ny, nz), jnp.float32),
             pltpu.VMEM((highs, 128), jnp.float32),
             pltpu.VMEM((n, per, 128), jnp.float32),
             pltpu.VMEM((n, per, 128), jnp.float32),
-            pltpu.SemaphoreType.DMA((6,)),
-            pltpu.SemaphoreType.DMA((10,)),
-            pltpu.SemaphoreType.DMA((10,)),
-            pltpu.SemaphoreType.DMA((10,)),
-            pltpu.SemaphoreType.DMA((10,)),
+            pltpu.SemaphoreType.DMA((7,)),
+            pltpu.SemaphoreType.DMA((PIECES, 10)),
+            pltpu.SemaphoreType.DMA((PIECES, 10)),
+            pltpu.SemaphoreType.DMA((PIECES, 2)),
+            pltpu.SemaphoreType.DMA((PIECES, 2)),
             pltpu.SemaphoreType.DMA((n,)),
             pltpu.SemaphoreType.DMA((n,)),
+            pltpu.VMEM(adjoint_in.shape, jnp.float32),
+            pltpu.SemaphoreType.DMA((PIECES,)),
+            pltpu.SemaphoreType.REGULAR((rounds, 2)),
         ],
         compiler_params=pltpu.CompilerParams(
-            collective_id=0, has_side_effects=True, vmem_limit_bytes=32 * 1024 * 1024
+            collective_id=0, has_side_effects=True, vmem_limit_bytes=60 * 1024 * 1024
         ),
         cost_estimate=pl.CostEstimate(
             flops=40_000_000, bytes_accessed=4_000_000, transcendentals=0

time: 38 us -> 31.3 us (0.82)
  local copies, waits for them, and re-layouts: 7.9 us -> 3.01 us
  Pallas kernels: 29.1 us -> 27.5 us
    unnamed x16 -> x4, local copies, waits for them, and re-layouts: 7.9 us -> 3.01 us
    pallas_call x1, Pallas kernels: 29.1 us -> 27.5 us  [body(): pl.pallas_call(functools.partial(kernel, n, low.bit_length() - 1), out_sh...]
where the time goes in v2:
time: 31.3 us; the launch traced here: 31.2 us
  Pallas kernels  27.5 us (88%)
  local copies, waits for them, and re-layouts  3.01 us (10%)
  between operations  0.65 us (2%)
    pallas_call x1, Pallas kernels, body(): pl.pallas_call(functools.partial(kernel, n, low.bit_length() - 1), out_sh...  27.5 us
    unnamed x4, local copies, waits for them, and re-layouts  3.01 us

profile of v2, /device:TPU:1, one launch (start us, length us, event | category | flops | bytes accessed | tf_op | source)
XLA Modules:
  0.0 31.2 jit_solution(17740529145947004636)
XLA Ops:
  0.6 27.5 %shard_map.86 = (f32[19,1,128,128]{3,2,1,0:T(8,128)}, f32[2,128]{1,0:T(2,128)}) custom-call(f32[19]{0:T(128)} %relax_hbm.1, f32[19,1,128,128]{3,2,1,0:T(8,128)} %adjoint_ref.1, f32[2,1,128,128]{3,2,1,0:T(8,128)} %density_ref.1, f32[2,3,1,128,128]{4,3,2,1,0:T(8,128)} %velocity_ref.1, s32[2,1,128,128]{3,2,1,0:T(8,128)} %links_ref.1, s32[1,128,128]{2,1,0:T(8,128)} %patch_ref.1, ...), custom_call_target="tpu_custom_call" | custom-call | flops 40000000 | bytes 4000000 | tf_op jit(solution)/shard_map/pallas_call | solution.py:497
  28.2 0.0 copy-start
  28.2 2.4 %copy.11 = f32[19,1,128,128]{3,2,1,0:T(8,128)} copy(f32[19,1,128,128]{3,2,1,0:T(8,128)} %get-tuple-element.8) | data formatting | bytes 2490368
  30.6 0.0 copy-done
  30.6 0.6 %copy.12 = f32[256]{0:T(256)} copy(f32[256]{0:T(256)S(1)} %bitcast.3) | data formatting | bytes 2048
Async XLA Ops:
  28.2 2.5 %copy-start = (f32[2,128]{1,0:T(2,128)S(1)}, f32[2,128]{1,0:T(2,128)}, u32[]{:S(2)}) copy-start(f32[2,128]{1,0:T(2,128)} %get-tuple-element.5) | copy-start | bytes 3076

commit v3 on v2

--- a/solution.py
+++ b/solution.py
@@ -247,8 +247,6 @@
     recv_two,
     send_sum,
     recv_sum,
-    result,
-    out_sem,
     met,
 ):
     me = lax.axis_index("span")
@@ -447,21 +445,13 @@
     lax.fori_loop(1, n, send, 0)
 
     def store_out(j, rows, inner, value):
-        result[j, 0, rows, :] = value
-
-    out_copies = []
+        out_ref[j, 0, rows, :] = value
+
     for i, end in enumerate(ends_out):
         for copy in copies_two[i]:
             copy.wait_recv()
         start = ends_out[i - 1] if i else 0
         collisions(0, second, PLACE, rims_two, store_out, start, end)
-        rows = pl.ds(start, end - start)
-        out_copies.append(
-            pltpu.make_async_copy(
-                result.at[:, :, rows, :], out_ref.at[:, :, rows, :], out_sem.at[i]
-            )
-        )
-        out_copies[-1].start()
 
     def collect(d, total):
         source = other(n - d)
@@ -478,8 +468,6 @@
     for copies in copies_one + copies_two:
         for copy in copies:
             copy.wait_send()
-    for copy in out_copies:
-        copy.wait()
 
 
 def body(n, adjoint_in, density, velocity, links, patch_map, owner, relax):
@@ -497,11 +485,11 @@
     adjoint, gradient = pl.pallas_call(
         functools.partial(kernel, n, low.bit_length() - 1),
         out_shape=(
-            jax.ShapeDtypeStruct(adjoint_in.shape, jnp.float32),
-            jax.ShapeDtypeStruct((per, 128), jnp.float32),
+            pltpu.VMEM(adjoint_in.shape, jnp.float32),
+            pltpu.VMEM((per, 128), jnp.float32),
         ),
         in_specs=[hbm] * 7,
-        out_specs=(hbm, vmem),
+        out_specs=(vmem, vmem),
         scratch_shapes=[
             pltpu.VMEM((19, padded, nz), jnp.float32),
             pltpu.VMEM((19, padded, nz), jnp.float32),
@@ -524,8 +512,6 @@
             pltpu.SemaphoreType.DMA((PIECES, 2)),
             pltpu.SemaphoreType.DMA((n,)),
             pltpu.SemaphoreType.DMA((n,)),
-            pltpu.VMEM(adjoint_in.shape, jnp.float32),
-            pltpu.SemaphoreType.DMA((PIECES,)),
             pltpu.SemaphoreType.REGULAR((rounds, 2)),
         ],
         compiler_params=pltpu.CompilerParams(

time: 31.3 us -> 28.6 us (0.914)
  local copies, waits for them, and re-layouts: 3.01 us -> 1.6 us
  Pallas kernels: 27.5 us -> 26.2 us
    unnamed x4 -> x2, local copies, waits for them, and re-layouts: 3.01 us -> 1.6 us
    pallas_call x1, Pallas kernels: 27.5 us -> 26.2 us  [body(): pl.pallas_call(functools.partial(kernel, n, low.bit_length() - 1), out_sh...]
where the time goes in v3:
time: 28.6 us; the launch traced here: 28.4 us
  Pallas kernels  26.2 us (92%)
  local copies, waits for them, and re-layouts  1.6 us (6%)
  between operations  0.64 us (2%)
    pallas_call x1, Pallas kernels, body(): pl.pallas_call(functools.partial(kernel, n, low.bit_length() - 1), out_sh...  26.2 us
    unnamed x2, local copies, waits for them, and re-layouts  1.6 us

profile of v3, /device:TPU:1, one launch (start us, length us, event | category | flops | bytes accessed | tf_op | source)
XLA Modules:
  0.0 28.4 jit_solution(17470922067861473655)
XLA Ops:
  0.6 26.2 %shard_map.86 = (f32[19,1,128,128]{3,2,1,0:T(8,128)S(1)}, f32[2,128]{1,0:T(2,128)S(1)}) custom-call(f32[19]{0:T(128)} %relax_hbm.1, f32[19,1,128,128]{3,2,1,0:T(8,128)} %adjoint_ref.1, f32[2,1,128,128]{3,2,1,0:T(8,128)} %density_ref.1, f32[2,3,1,128,128]{4,3,2,1,0:T(8,128)} %velocity_ref.1, s32[2,1,128,128]{3,2,1,0:T(8,128)} %links_ref.1, ...), custom_call_target="tpu_custom_call" | custom-call | flops 40000000 | bytes 4000000 | tf_op jit(solution)/shard_map/pallas_call | solution.py:485
  26.8 1.0 %copy.11 = f32[19,1,128,128]{3,2,1,0:T(8,128)} copy(f32[19,1,128,128]{3,2,1,0:T(8,128)S(1)} %get-tuple-element.6) | data formatting | bytes 2490368
  27.9 0.6 %copy.12 = f32[256]{0:T(256)} copy(f32[256]{0:T(256)S(1)} %bitcast.2) | data formatting | bytes 2048

commit v4 on v3

--- a/solution.py
+++ b/solution.py
@@ -257,19 +257,16 @@
     def other(d):
         return lax.rem(me + d, n)
 
+    pairs = [(relax_hbm, relax_ref)]
+    pairs += [(adjoint_ref.at[j, 0], first.at[j, pl.ds(PAD, ny), :]) for j in range(19)]
+    pairs += [(links_ref.at[i, 0], bits.at[i]) for i in range(2)]
+    for level in (1, 0):
+        pairs += [(velocity_ref.at[level, i, 0], flow.at[level, i]) for i in range(3)]
+        pairs.append((density_ref.at[level, 0], rho.at[level]))
+    pairs += [(patch_ref.at[0], patch), (owner_ref, owner)]
     loads = [
         pltpu.make_async_copy(source, target, local_sem.at[i])
-        for i, (source, target) in enumerate(
-            (
-                (adjoint_ref.at[:, 0], first.at[:, pl.ds(PAD, ny), :]),
-                (links_ref.at[:, 0], bits),
-                (velocity_ref.at[:, :, 0], flow),
-                (density_ref.at[:, 0], rho),
-                (patch_ref.at[0], patch),
-                (owner_ref, owner),
-                (relax_hbm, relax_ref),
-            )
-        )
+        for i, (source, target) in enumerate(pairs)
     ]
     for load in loads:
         load.start()
@@ -359,7 +356,7 @@
             wall[rows, :] = wall[rows, :] + value if add else value
             return carry
 
-        lax.fori_loop(0, chunks, step, 0)
+        lax.fori_loop(0, chunks, step, 0, unroll=4)
 
     def collisions(level, populations, place, rims, store, begin, end):
         def step(i, carry):
@@ -384,7 +381,7 @@
                 store(j, rows, inner, value)
             return carry
 
-        lax.fori_loop(begin // ROWS, end // ROWS, step, 0)
+        lax.fori_loop(begin // ROWS, end // ROWS, step, 0, unroll=4)
 
     def store_second(j, rows, inner, value):
         second[PLACE[j], inner, :] = value
@@ -505,7 +502,7 @@
             pltpu.VMEM((highs, 128), jnp.float32),
             pltpu.VMEM((n, per, 128), jnp.float32),
             pltpu.VMEM((n, per, 128), jnp.float32),
-            pltpu.SemaphoreType.DMA((7,)),
+            pltpu.SemaphoreType.DMA((32,)),
             pltpu.SemaphoreType.DMA((PIECES, 10)),
             pltpu.SemaphoreType.DMA((PIECES, 10)),
             pltpu.SemaphoreType.DMA((PIECES, 2)),

time: 28.6 us -> 27.8 us (0.972); the launches traced: 28.4 us -> 27.3 us
  Pallas kernels: 26.2 us -> 25 us
    pallas_call x1, Pallas kernels: 26.2 us -> 25 us  [body(): pl.pallas_call(functools.partial(kernel, n, low.bit_length() - 1), out_sh...]
where the time goes in v4:
time: 27.8 us; the launch traced here: 27.3 us
  Pallas kernels  25 us (90%)
  local copies, waits for them, and re-layouts  1.6 us (6%)
  between operations  0.64 us (2%)
    pallas_call x1, Pallas kernels, body(): pl.pallas_call(functools.partial(kernel, n, low.bit_length() - 1), out_sh...  25 us
    unnamed x2, local copies, waits for them, and re-layouts  1.6 us

profile of v4, /device:TPU:1, one launch (start us, length us, event | category | flops | bytes accessed | tf_op | source)
XLA Modules:
  0.0 27.3 jit_solution(5445451903001254278)
XLA Ops:
  0.6 25.0 %shard_map.86 = (f32[19,1,128,128]{3,2,1,0:T(8,128)S(1)}, f32[2,128]{1,0:T(2,128)S(1)}) custom-call(f32[19]{0:T(128)} %relax_hbm.1, f32[19,1,128,128]{3,2,1,0:T(8,128)} %adjoint_ref.1, f32[2,1,128,128]{3,2,1,0:T(8,128)} %density_ref.1, f32[2,3,1,128,128]{4,3,2,1,0:T(8,128)} %velocity_ref.1, s32[2,1,128,128]{3,2,1,0:T(8,128)} %links_ref.1, ...), custom_call_target="tpu_custom_call" | custom-call | flops 40000000 | bytes 4000000 | tf_op jit(solution)/shard_map/pallas_call | solution.py:482
  25.7 1.0 %copy.11 = f32[19,1,128,128]{3,2,1,0:T(8,128)} copy(f32[19,1,128,128]{3,2,1,0:T(8,128)S(1)} %get-tuple-element.6) | data formatting | bytes 2490368
  26.7 0.6 %copy.12 = f32[256]{0:T(256)} copy(f32[256]{0:T(256)S(1)} %bitcast.2) | data formatting | bytes 2048

commit v5 on v4

--- a/solution.py
+++ b/solution.py
@@ -408,7 +408,7 @@
         return total + one_hot_sums(patch[rows, :], wall[rows, :], 7, owner.shape[0])
 
     highs = owner.shape[0]
-    total = lax.fori_loop(0, chunks, by_patch, jnp.zeros((3 * highs, 128), jnp.float32))
+    total = lax.fori_loop(0, chunks, by_patch, jnp.zeros((3 * highs, 128), jnp.float32), unroll=2)
     sums[...] = total[:highs] + (total[highs : 2 * highs] + total[2 * highs :])
 
     targets = outgoing.shape[0] * outgoing.shape[1]
@@ -418,7 +418,7 @@
         return total + one_hot_sums(owner[rows, :], sums[rows, :], low_bits, targets)
 
     total = lax.fori_loop(
-        0, highs // ROWS, by_owner, jnp.zeros((3 * targets, 128), jnp.float32)
+        0, highs // ROWS, by_owner, jnp.zeros((3 * targets, 128), jnp.float32), unroll=True
     )
     placed = total[:targets] + (total[targets : 2 * targets] + total[2 * targets :])
     per = outgoing.shape[1]
@@ -439,7 +439,7 @@
         sum_copy(d, me).start()
         return carry
 
-    lax.fori_loop(1, n, send, 0)
+    lax.fori_loop(1, n, send, 0, unroll=n < 32)
 
     def store_out(j, rows, inner, value):
         out_ref[j, 0, rows, :] = value
@@ -455,13 +455,13 @@
         sum_copy(d, source).wait_recv()
         return total + incoming[source]
 
-    gradient_ref[...] = lax.fori_loop(1, n, collect, outgoing[me])
+    gradient_ref[...] = lax.fori_loop(1, n, collect, outgoing[me], unroll=n < 32)
 
     def sent(d, carry):
         sum_copy(d, me).wait_send()
         return carry
 
-    lax.fori_loop(1, n, sent, 0)
+    lax.fori_loop(1, n, sent, 0, unroll=n < 32)
     for copies in copies_one + copies_two:
         for copy in copies:
             copy.wait_send()

time: 27.8 us -> 26.7 us (0.960); the launches traced: 27.3 us -> 26.5 us
  Pallas kernels: 25 us -> 24.3 us
    pallas_call x1, Pallas kernels: 25 us -> 24.3 us  [body(): pl.pallas_call(functools.partial(kernel, n, low.bit_length() - 1), out_sh...]
where the time goes in v5:
time: 26.7 us; the launch traced here: 26.5 us
  Pallas kernels  24.3 us (91%)
  local copies, waits for them, and re-layouts  1.6 us (6%)
  between operations  0.64 us (2%)
    pallas_call x1, Pallas kernels, body(): pl.pallas_call(functools.partial(kernel, n, low.bit_length() - 1), out_sh...  24.3 us
    unnamed x2, local copies, waits for them, and re-layouts  1.6 us

profile of v5, /device:TPU:1, one launch (start us, length us, event | category | flops | bytes accessed | tf_op | source)
XLA Modules:
  0.0 26.5 jit_solution(3348871357554286532)
XLA Ops:
  0.6 24.3 %shard_map.86 = (f32[19,1,128,128]{3,2,1,0:T(8,128)S(1)}, f32[2,128]{1,0:T(2,128)S(1)}) custom-call(f32[19]{0:T(128)} %relax_hbm.1, f32[19,1,128,128]{3,2,1,0:T(8,128)} %adjoint_ref.1, f32[2,1,128,128]{3,2,1,0:T(8,128)} %density_ref.1, f32[2,3,1,128,128]{4,3,2,1,0:T(8,128)} %velocity_ref.1, s32[2,1,128,128]{3,2,1,0:T(8,128)} %links_ref.1, ...), custom_call_target="tpu_custom_call" | custom-call | flops 40000000 | bytes 4000000 | tf_op jit(solution)/shard_map/pallas_call | solution.py:482
  24.9 1.0 %copy.11 = f32[19,1,128,128]{3,2,1,0:T(8,128)} copy(f32[19,1,128,128]{3,2,1,0:T(8,128)S(1)} %get-tuple-element.6) | data formatting | bytes 2490368
  25.9 0.6 %copy.12 = f32[256]{0:T(256)} copy(f32[256]{0:T(256)S(1)} %bitcast.2) | data formatting | bytes 2048
